TPU v7x, 32 devices: a whole 2x2x4 slice. The times are simulated.
32 devices in a mesh: sec: 4 (over z), blk: 8 (over y, x, core).
Axes of the slice: x: 2, y: 2, z: 4, core: 2. Of those that a mesh axis runs over, the one named last changes fastest.
Arguments:
- wavefunction: bfloat16 [4, 96, 128, 128], P('sec', 'blk')
- left_env: bfloat16 [4, 20, 96, 128, 128], P('sec', None, 'blk')
- right_env: bfloat16 [4, 20, 96, 128, 128], P('sec', None, 'blk')
- row_offset: int32 [4, 12], P('sec'), may hold values from 0 to 7, as said below
- sector_dims: int32 [4, 96, 2], P('sec', 'blk'), may hold values from 64 to 128
- trunc_ranks: int32 [4, 96], P('sec', 'blk'), may hold values from 32 to 128
Outputs:
- state_new: bfloat16 [4, 96, 128, 128], P('sec', 'blk')
- hstate_new: bfloat16 [4, 96, 128, 128], P('sec', 'blk')
- energy: float32 [4], P('sec')
- next_left: bfloat16 [4, 20, 96, 128, 128], P('sec', None, 'blk')
Inputs may be any that keep to these rules, and one draw needn't show every extreme that they name: The sector with up-charge u and down-charge e is stored in slot u of device (e + row_offset[u]) mod 8; in every section the offsets of some two adjacent up-charges differ by 8 / 2 modulo 8.
All inputs are finite; a program needn't handle non-finite values.
Results may differ from a plain program's by a relative error of at most 0.0067.
Values may be sent and summed in bfloat16 or wider, within the bound.
No kernel may reach another device: no remote copies, remote signals or barrier semaphores. Data moves between devices by JAX's collectives and lax.ppermute only.
A program may use at most 128 MiB of HBM per device.

v0:
```python
import jax
import jax.numpy as jnp
from jax import lax
from jax.sharding import PartitionSpec as P


def passed_along(value, axis, by):
    length = lax.axis_size(axis)
    pairs = [(i, i + by) for i in range(length) if 0 <= i + by < length]
    return lax.ppermute(value, axis, pairs)


def route_blocks(state, offsets, device, nblk):
    count = state.shape[0]
    up_val = jnp.arange(count, dtype=jnp.int32)
    prev_off = jnp.roll(offsets, 1)
    next_off = jnp.roll(offsets, -1)
    down_val = (device - offsets) % nblk
    exists = [up_val >= 1, up_val <= count - 2, down_val >= 1, down_val <= nblk - 2]
    whole = lax.all_gather(state, "blk", axis=0, tiled=True)
    row_lo = jnp.clip(up_val - 1, 0, count - 1)
    row_hi = jnp.clip(up_val + 1, 0, count - 1)
    indices = [
        (down_val + prev_off) % nblk * count + row_lo,
        (down_val + next_off) % nblk * count + row_hi,
        (device - 1) % nblk * count + up_val,
        (device + 1) % nblk * count + up_val,
    ]
    picked = [jnp.take(whole, entry, axis=0) for entry in indices]
    result = [state]
    for ctype in range(4):
        result.append(
            jnp.where(exists[ctype][:, None, None], picked[ctype], jnp.zeros_like(picked[ctype]))
        )
    return result


def apply_ham(state, lenv, renv, mask, offsets, device, nblk):
    blocks = route_blocks(state, offsets, device, nblk)
    total = jnp.zeros(state.shape, jnp.float32)
    for ctype in range(5):
        inner = jnp.einsum(
            "wtab,tbc->wtac", lenv[ctype::5], blocks[ctype], preferred_element_type=jnp.float32
        ).astype(jnp.bfloat16)
        total = total + jnp.einsum(
            "wtac,wtdc->tad", inner, renv[ctype::5], preferred_element_type=jnp.float32
        )
    return total * mask


def shards(wavefunction, left_env, right_env, row_offset, sector_dims, trunc_ranks):
    start = wavefunction[0]
    lenv = left_env[0]
    renv = right_env[0]
    offsets = row_offset[0]
    dims = sector_dims[0]
    kept_cols = trunc_ranks[0]
    count = start.shape[0]
    width = start.shape[1]
    channels = lenv.shape[0]
    nblk = lax.axis_size("blk")
    device = lax.axis_index("blk")
    cells = float(count * nblk * width * width)
    lines = jnp.arange(width, dtype=jnp.int32)
    mask_on = (lines[None, :, None] < dims[:, 0][:, None, None]) & (
        lines[None, None, :] < dims[:, 1][:, None, None]
    )
    mask = mask_on.astype(jnp.float32)
    vzero = jnp.where(mask_on, start, jnp.zeros_like(start))
    hzero = apply_ham(vzero, lenv, renv, mask, offsets, device, nblk)
    vzero_f = vzero.astype(jnp.float32)
    nzero_part = jnp.sum(vzero_f * vzero_f)
    pzero_part = jnp.sum(vzero_f * hzero)
    nzero, pzero = lax.psum((nzero_part, pzero_part), "blk")
    scale = jnp.sqrt(cells / nzero)
    uzero = vzero_f * scale
    huzero = hzero * scale
    a_zero = pzero / nzero
    resid = huzero - a_zero * uzero
    squares = lax.psum(jnp.sum(resid * resid), "blk") / cells
    beta = jnp.sqrt(squares + 1e-06)
    vone = (resid / beta).astype(jnp.bfloat16)
    hone = apply_ham(vone, lenv, renv, mask, offsets, device, nblk)
    a_one = lax.psum(jnp.sum(vone.astype(jnp.float32) * hone), "blk") / cells
    half_gap = (a_zero - a_one) / 2.0
    ritz = (a_zero + a_one) / 2.0 - jnp.sqrt(half_gap * half_gap + beta * beta)
    gap_val = ritz - a_zero
    length = jnp.sqrt(beta * beta + gap_val * gap_val)
    xcoef = beta / length
    ycoef = gap_val / length
    state_new = (xcoef * uzero + ycoef * vone.astype(jnp.float32)).astype(jnp.bfloat16)
    hstate_new = (xcoef * huzero + ycoef * hone).astype(jnp.bfloat16)
    kept_on = lines[None, None, :] < kept_cols[:, None, None]
    kept = jnp.where(kept_on, state_new, jnp.zeros_like(state_new))
    kept_src = route_blocks(kept, offsets, device, nblk)
    pieces = []
    for ctype in range(5):
        inner = jnp.einsum(
            "wtab,tbc->wtac", lenv[ctype::5], kept_src[ctype], preferred_element_type=jnp.float32
        ).astype(jnp.bfloat16)
        piece = jnp.einsum(
            "tba,wtbc->wtac", kept, inner, preferred_element_type=jnp.float32
        ).astype(jnp.bfloat16)
        pieces.append(piece)
    stacked = jnp.stack(pieces, axis=1).reshape((channels, count, width, width))
    received = passed_along(stacked, "sec", 1)
    first_section = lax.axis_index("sec") == 0
    next_left = jnp.where(first_section, lenv, received)
    return (state_new[None], hstate_new[None], jnp.reshape(ritz, (1,)), next_left[None])


def solution(mesh):
    placed = (
        P("sec", "blk", None, None),
        P("sec", None, "blk", None, None),
        P("sec", None, "blk", None, None),
        P("sec", None),
        P("sec", "blk", None),
        P("sec", "blk"),
    )
    return jax.shard_map(
        shards,
        mesh=mesh,
        in_specs=placed,
        out_specs=(
            P("sec", "blk", None, None),
            P("sec", "blk", None, None),
            P("sec"),
            P("sec", None, "blk", None, None),
        ),
        check_vma=False,
    )
```

profile of v0, /device:TPU:8, one launch (start us, length us, event | category | flops | bytes accessed | tf_op | source)
XLA Modules:
  0.0 453.3 jit_solution(3420859657352870947)
XLA Ops:
  8.0 2.0 and_select_fusion
  10.3 1.3 fusion.370
  13.0 1.4 compare_and_fusion.2
  14.5 11.6 %copy_bitcast_fusion = (bf16[20,12,128,128]{3,2,0,1:T(8,128)(2,1)}, bf16[20,12,128,128]{3,2,0,1:T(8,128)(2,1)}) fusion(bf16[1,20,12,128,128]{4,3,2,1,0:T(8,128)(2,1)} %param.10, bf16[1,20,12,128,128]{4,3,2,1,0:T(8,128)(2,1)} %param.9), kind=kLoop, calls=%fused_computation.12 | loop fusion | bytes 31457280 | tf_op jit(solution)/shard_map/squeeze | solution.py:54
  26.1 2.9 fusion.45
  29.0 15.0 %all-gather.4.cloned.1.call-done = bf16[96,128,128]{2,1,0:T(8,128)(2,1)} async-done(((bf16[12,128,128]{2,1,0:T(8,128)(2,1)}), bf16[96,128,128]{2,1,0:T(8,128)(2,1)}) %all-gather.4.cloned.1.call-update) | async-done | bytes 3145744 | tf_op jit(solution)/shard_map/all_gather | solution.py:20
  44.0 2.5 gather_fusion
  46.5 3.4 fusion.140
  49.9 2.5 gather_fusion.1
  52.4 3.4 fusion.135
  55.8 2.5 gather_fusion.2
  58.3 3.4 fusion.130
  61.7 2.5 gather_fusion.3
  64.2 4.0 fusion.181
  68.2 13.7 %all-reduce = (f32[]{:T(128)}, f32[]{:T(128)}) all-reduce(f32[]{:T(128)} %get-tuple-element.10, f32[]{:T(128)} %get-tuple-element.9), channel_id=1, replica_groups=mesh['sec'=4,'blk'=8] {'blk'}, use_global_device_ids=true, to_apply=%region_3.5 | all-reduce | flops 2 | bytes 16 | tf_op jit(solution)/shard_map/psum | solution.py:74
  84.0 0.9 multiply_reduce_fusion
  84.9 12.4 %psum.30 = f32[]{:T(128)} all-reduce(f32[]{:T(128)} %multiply_reduce_fusion), channel_id=1, replica_groups=mesh['sec'=4,'blk'=8] {'blk'}, use_global_device_ids=true, to_apply=%region_5.7 | all-reduce | flops 1 | bytes 8 | tf_op jit(solution)/shard_map/psum | solution.py:80
  98.0 1.1 divide_convert_fusion
  99.5 3.0 fusion.70
  102.5 29.1 %all-gather.6.cloned.1.call-done = bf16[96,128,128]{2,1,0:T(8,128)(2,1)} async-done(((bf16[12,128,128]{2,1,0:T(8,128)(2,1)}), bf16[96,128,128]{2,1,0:T(8,128)(2,1)}) %all-gather.6.cloned.1.call-update) | async-done | bytes 3145744 | tf_op jit(solution)/shard_map/all_gather | solution.py:20
  131.6 2.5 gather_fusion.4
  134.2 4.3 fusion.115
  138.4 2.5 gather_fusion.5
  141.0 3.6 fusion.110
  144.5 2.5 gather_fusion.6
  147.1 4.3 fusion.105
  151.4 2.5 gather_fusion.7
  153.9 4.1 fusion.180
  158.0 13.9 %psum.31 = f32[]{:T(128)} all-reduce(f32[]{:T(128)} %get-tuple-element.29), channel_id=1, replica_groups=mesh['sec'=4,'blk'=8] {'blk'}, use_global_device_ids=true, to_apply=%region_7.9 | all-reduce | flops 1 | bytes 8 | tf_op jit(solution)/shard_map/psum | solution.py:84
  172.8 1.1 broadcast_select_fusion
  173.9 3.8 bitcast_dynamic-update-slice_fusion.4
  177.7 28.7 %all-gather.8.cloned.1.call-done = bf16[96,128,128]{2,1,0:T(8,128)(2,1)} async-done(((bf16[12,128,128]{2,1,0:T(8,128)(2,1)}), bf16[96,128,128]{2,1,0:T(8,128)(2,1)}) %all-gather.8.cloned.1.call-update) | async-done | bytes 3145744 | tf_op jit(solution)/shard_map/all_gather | solution.py:20
  206.4 2.5 gather_fusion.8
  208.9 3.9 bitcast_dynamic-update-slice_fusion.3
  212.8 2.5 gather_fusion.9
  215.3 3.9 bitcast_dynamic-update-slice_fusion.2
  219.3 2.5 gather_fusion.10
  221.8 3.9 bitcast_dynamic-update-slice_fusion.1
  225.7 2.5 gather_fusion.11
  228.2 3.9 bitcast_dynamic-update-slice_fusion
  232.1 10.7 %copy.40 = bf16[4,5,12,128,128]{4,3,2,1,0:T(8,128)(2,1)} copy(bf16[4,5,12,128,128]{3,4,0,2,1:T(8,128)(2,1)} %bitcast_dynamic-update-slice_fusion) | data formatting | bytes 15728640 | tf_op jit(solution)/shard_map/stack | solution.py:105
  242.8 9.9 %copy.41 = bf16[20,12,128,128]{3,2,0,1:T(8,128)(2,1)} copy(bf16[20,12,128,128]{3,2,1,0:T(8,128)(2,1)} %bitcast.313) | data formatting | bytes 15728640 | tf_op jit(solution)/shard_map/reshape | solution.py:105
  252.7 3.4 collective-permute-start
  256.1 1.1 fusion.314
  257.2 0.9 fusion.183
  258.1 168.2 %collective-permute-done = bf16[20,12,128,128]{3,2,0,1:T(8,128)(2,1)} collective-permute-done((bf16[20,12,128,128]{3,2,0,1:T(8,128)(2,1)}, bf16[20,12,128,128]{3,2,0,1:T(8,128)(2,1)}, u32[]{:S(2)}, u32[]{:S(2)}) %collective-permute-start) | collective-permute-done | bytes 7864352 | tf_op jit(solution)/shard_map/ppermute | solution.py:10
  426.3 9.4 %select_bitcast_fusion = bf16[1,20,12,128,128]{4,3,1,2,0:T(8,128)(2,1)} fusion(bf16[20,12,128,128]{3,2,0,1:T(8,128)(2,1)} %collective-permute-done, pred[]{:T(512)S(6)} %eq.20, bf16[1,20,12,128,128]{4,3,2,1,0:T(8,128)(2,1)} %param.9), kind=kLoop, calls=%fused_computation.14 | loop fusion | flops 3932160 | bytes 23592960 | tf_op jit(solution)/shard_map/broadcast_in_dim | solution.py:109
  435.7 9.9 %copy.42 = bf16[1,20,12,128,128]{4,3,2,1,0:T(8,128)(2,1)} copy(bf16[1,20,12,128,128]{4,3,1,2,0:T(8,128)(2,1)} %select_bitcast_fusion) | data formatting | bytes 15728640
  (29 shorter events, 2.8 us)
Async XLA Ops:
  7.2 36.8 %all-gather.4.cloned.1.call-start = ((), (), s32[]{:S(2)}) async-start(), calls=%async_computation | async-start | bytes 3538944 | tf_op jit(solution)/shard_map/all_gather | solution.py:20
  10.1 121.5 %all-gather.6.cloned.1.call-start = ((), (), s32[]{:S(2)}) async-start(), calls=%async_computation.1 | async-start | bytes 3538944 | tf_op jit(solution)/shard_map/all_gather | solution.py:20
  14.4 11.6 %copy-start.2 = (bf16[12,128,128]{2,1,0:T(8,128)(2,1)S(1)}, bf16[12,128,128]{2,1,0:T(8,128)(2,1)}, u32[]{:S(2)}) copy-start(bf16[12,128,128]{2,1,0:T(8,128)(2,1)} %and_select_fusion) | copy-start | bytes 1179652
  64.2 19.8 %copy-start = (bf16[1,12,128,128]{3,2,1,0:T(8,128)(2,1)S(1)}, bf16[1,12,128,128]{3,2,1,0:T(8,128)(2,1)}, u32[]{:S(2)}) copy-start(bf16[1,12,128,128]{3,2,1,0:T(8,128)(2,1)} %param.8) | copy-start | bytes 1179652
  68.2 31.2 %copy-start.4 = (s32[1,12]{1,0:T(1,128)S(1)}, s32[1,12]{1,0:T(1,128)}, u32[]{:S(2)}) copy-start(s32[1,12]{1,0:T(1,128)} %param.13) | copy-start | bytes 148
  99.1 107.2 %all-gather.8.cloned.1.call-start = ((), (), s32[]{:S(2)}) async-start(), calls=%async_computation.2 | async-start | bytes 3538944 | tf_op jit(solution)/shard_map/all_gather | solution.py:20
  147.1 6.9 %copy-start.1 = (bf16[12,128,128]{2,1,0:T(8,128)(2,1)S(1)}, bf16[12,128,128]{2,1,0:T(8,128)(2,1)}, u32[]{:S(2)}) copy-start(bf16[12,128,128]{2,1,0:T(8,128)(2,1)} %divide_convert_fusion) | copy-start | bytes 1179652
  173.9 35.0 %copy-start.3 = (bf16[12,128,128]{2,1,0:T(8,128)(2,1)S(1)}, bf16[12,128,128]{2,1,0:T(8,128)(2,1)}, u32[]{:S(2)}) copy-start(bf16[12,128,128]{2,1,0:T(8,128)(2,1)} %broadcast_select_fusion) | copy-start | bytes 1179652
  252.7 173.6 %collective-permute-start = (bf16[20,12,128,128]{3,2,0,1:T(8,128)(2,1)}, bf16[20,12,128,128]{3,2,0,1:T(8,128)(2,1)}, u32[]{:S(2)}, u32[]{:S(2)}) collective-permute-start(bf16[20,12,128,128]{3,2,0,1:T(8,128)(2,1)} %copy.41), channel_id=1, source_target_pairs={{0,8},{8,16},{16,24},{1,9},{9,17},{17,25},{2,10},{10,18},{18,26},{... | collective-permute-start | bytes 23592968 | tf_op jit(solution)/shard_map/ppermute | solution.py:10
Sparse Core Ops, SparseCore 0:
  10.5 33.4 all-gather.3
  99.3 32.3 all-gather.5
  174.0 32.3 all-gather.7
where the time goes:
time: 455 us; the launch traced here: 453 us
  waiting for transfers between devices  241 us (53%)
  local copies, waits for them, and re-layouts  75.1 us (17%)
  matrix products  55.8 us (12%)
  blocking collectives  40.1 us (9%)
  other arithmetic  18.8 us (4%)
  between operations  18.8 us (4%)
    ppermute x1, waiting for transfers between devices, passed_along(): return lax.ppermute(value, axis, pairs)  168 us
    all_gather x3, waiting for transfers between devices, route_blocks(): whole = lax.all_gather(state, 'blk', axis=0, tiled=True)  72.7 us
    dot_general x10, matrix products, apply_ham(): jnp.einsum('wtac,wtdc->tad', inner, renv[ctype::5], preferred_element_typ...  36.4 us
    gather x12, local copies, waits for them, and re-layouts, route_blocks(): picked = [jnp.take(whole, entry, axis=0) for entry in indices]  30.1 us
    dot_general x5, matrix products, shards(): jnp.einsum('tba,wtbc->wtac', kept, inner, preferred_element_type=jnp.floa...  19.5 us
    psum x1, blocking collectives, shards(): a_one = lax.psum(jnp.sum(vone.astype(jnp.float32) * hone), 'blk') / cells  13.9 us
    psum x1, blocking collectives, shards(): nzero, pzero = lax.psum((nzero_part, pzero_part), 'blk')  13.7 us
    psum x1, blocking collectives, shards(): squares = lax.psum(jnp.sum(resid * resid), 'blk') / cells  12.4 us
  transfers between devices with their start and end apart: 4, of which 4 were waited for; matrix products, arithmetic and copies ran while one was open for 6% of the time, Pallas kernels for 0%

commit v1 on v0

v1 whole, which is shorter than its diff:
```python
import functools

import jax
import jax.numpy as jnp
from jax import lax
from jax.experimental import pallas as pl
from jax.experimental.pallas import tpu as pltpu
from jax.sharding import PartitionSpec as P

GROUPS = 5
EARLY = (1, 2)
LATE = (0, 3, 4)
EXTRA = 16
SLACK = 128
VMEM = 56 * 1024 * 1024
F32 = jnp.float32
BF16 = jnp.bfloat16


def params():
    return pltpu.CompilerParams(vmem_limit_bytes=VMEM)


def exchange(value, bit):
    length = lax.axis_size("blk")
    return lax.ppermute(value, "blk", [(i, i ^ bit) for i in range(length)])


def onward(value):
    length = lax.axis_size("sec")
    return lax.ppermute(value, "sec", [(i, i + 1) for i in range(length - 1)])


def gathered(value):
    nblk = lax.axis_size("blk")
    if nblk == 8:
        rows = value.shape[0]
        half = rows // 2 // 16 * 16
        four, two, one = exchange(value, 4), exchange(value, 2), exchange(value, 1)
        six_a, six_b = exchange(two[:half], 4), exchange(four[half:], 2)
        three, five = exchange(two, 1), exchange(four, 1)
        seven_a, seven_b = exchange(six_a, 1), exchange(six_b, 1)
        return [
            (value, 0, 0), (one, 1, 0), (two, 2, 0), (three, 3, 0), (four, 4, 0), (five, 5, 0),
            (six_a, 6, 0), (six_b, 6, half), (seven_a, 7, 0), (seven_b, 7, half),
        ]
    held = {0: value}
    bit = 1
    while bit < nblk:
        held.update({place | bit: exchange(rows, bit) for place, rows in list(held.items())})
        bit *= 2
    return [(held[place], place, 0) for place in range(nblk)]


def extras_of(pieces, nblk, body):
    found = [None] * nblk
    for rows, place, first in pieces:
        if first + rows.shape[0] == body + EXTRA:
            found[place] = rows[rows.shape[0] - EXTRA :]
    return jnp.stack(found)


def load_pieces(places, refs, scratch, sem):
    copies = []
    for (place, first), ref in zip(places, refs):
        copies.append(
            pltpu.make_async_copy(ref, scratch.at[place, pl.ds(first, ref.shape[0])], sem.at[len(copies)])
        )
    for copy in copies:
        copy.start()
    return copies


def block_of(scratch, entry, count, width):
    place = entry // count
    slot = entry - place * count
    return scratch[place, pl.ds(pl.multiple_of(slot * width, width), width), :]


def ham_sum(x, lref, rref):
    kinds = lref.shape[0] // GROUPS
    zero = jnp.zeros_like(x[0])
    width = zero.shape[0]
    total = jnp.zeros((width, width), F32)
    flip = (((1,), (1,)), ((), ()))
    for c0, c1 in ((0, 1), (2, 3)):
        both = jnp.concatenate(
            [jnp.concatenate([x[c0], zero], 1), jnp.concatenate([zero, x[c1]], 1)], 0
        )
        left = jnp.concatenate(
            [jnp.concatenate([lref[GROUPS * k + c0, 0], lref[GROUPS * k + c1, 0]], 1) for k in range(kinds)], 0
        )
        inner = jnp.dot(left, both, preferred_element_type=F32).astype(BF16)
        for k in range(kinds):
            right = jnp.concatenate([rref[GROUPS * k + c0, 0], rref[GROUPS * k + c1, 0]], 1)
            total += lax.dot_general(
                inner[width * k : width * (k + 1)], right, flip, preferred_element_type=F32
            )
    left = jnp.concatenate([lref[GROUPS * k + 4, 0] for k in range(kinds)], 0)
    inner = jnp.dot(left, x[4], preferred_element_type=F32).astype(BF16)
    inner = jnp.concatenate([inner[width * k : width * (k + 1)] for k in range(kinds)], 1)
    right = jnp.concatenate([rref[GROUPS * k + 4, 0] for k in range(kinds)], 1)
    return total + lax.dot_general(inner, right, flip, preferred_element_type=F32)


def inside(rows, cols, shape):
    row = lax.broadcasted_iota(jnp.int32, shape, 0)
    col = lax.broadcasted_iota(jnp.int32, shape, 1)
    return (row < rows) & (col < cols)


def total_of(value):
    return jnp.sum(jnp.sum(value, axis=0, keepdims=True), axis=1, keepdims=True)


def first_kernel(places, count, idx, there, dims, *refs):
    pieces = refs[: len(places)]
    lref, rref, href, payload, held, ext, sem = refs[len(places) :]
    t = pl.program_id(0)
    width = href.shape[1]

    @pl.when(t == 0)
    def _():
        copies = load_pieces(places, pieces, held, sem)
        ext[...] = jnp.zeros_like(ext)
        for copy in copies:
            copy.wait()

    x = []
    for c in range(GROUPS):
        block = block_of(held, idx[c, t], count, width)
        x.append(jnp.where(there[c, t] > 0, block, jnp.zeros_like(block)))
    total = ham_sum(x, lref, rref)
    h = jnp.where(inside(dims[t, 0], dims[t, 1], (width, width)), total, 0.0)
    href[0] = h
    v = x[0].astype(F32)
    norm, num = total_of(v * v), total_of(v * h)
    alpha = jnp.where(norm > 1e-30, num / jnp.maximum(norm, 1e-30), 0.0).astype(BF16).astype(F32)
    payload[pl.ds(pl.multiple_of(t * width, width), width), :] = (h - alpha * v).astype(BF16)
    row = lax.broadcasted_iota(jnp.int32, ext.shape, 0)
    lane = lax.broadcasted_iota(jnp.int32, ext.shape, 1)
    now = jnp.where(row == t, alpha, ext[...])
    now = now + jnp.where(row == count, norm, 0.0) + jnp.where(row == count + 1, num, 0.0)
    ext[...] = now

    @pl.when(t == count - 1)
    def _():
        high = now.astype(BF16).astype(F32)
        rest = now - high
        mid = rest.astype(BF16).astype(F32)
        low = rest - mid
        split = jnp.where(lane == 0, high, jnp.where(lane == 1, mid, jnp.where(lane == 2, low, 0.0)))
        payload[pl.ds(count * width, EXTRA), :] = jnp.where(row < count, now, split).astype(BF16)


def second_kernel(places, count, cells, idx, there, dims, *refs):
    n = len(places)
    vpieces, rpieces = refs[:n], refs[n : 2 * n]
    lref, rref, gref, sums, vsrc, wsrc, vheld, rheld, ext, vsem, rsem = refs[2 * n :]
    t = pl.program_id(0)
    width = gref.shape[1]
    nblk = vheld.shape[0]
    srow = lax.broadcasted_iota(jnp.int32, sums.shape, 0)

    @pl.when(t == 0)
    def _():
        copies = load_pieces(places, vpieces, vheld, vsem) + load_pieces(places, rpieces, rheld, rsem)
        for copy in copies:
            copy.wait()
        both = jnp.zeros((EXTRA, 128), F32)
        for place in range(nblk):
            part = rheld[place, pl.ds(count * width, EXTRA), :].astype(F32)
            ext[pl.ds(place * EXTRA, EXTRA), :] = part
            both = both + part
        both = jnp.sum(both, axis=1, keepdims=True)
        norm, num = both[count : count + 1], both[count + 1 : count + 2]
        sums[...] = jnp.where(srow == 2, num / norm, jnp.where(srow == 3, jnp.sqrt(cells / norm), 0.0))

    a_zero, scale = sums[2:3, :], sums[3:4, :]
    x = []
    squares = None
    for c in range(GROUPS):
        entry = idx[c, t]
        on = there[c, t] > 0
        place = entry // count
        v = block_of(vheld, entry, count, width)
        r = block_of(rheld, entry, count, width).astype(F32)
        alpha = ext[pl.ds(place * EXTRA + (entry - place * count), 1), :]
        w = scale * (r + (alpha - a_zero) * v.astype(F32))
        if c == 0:
            squares = total_of(w * w)
        w = jnp.where(on, w, 0.0).astype(BF16)
        x.append(w)
        if c in LATE:
            vsrc[LATE.index(c), 0] = jnp.where(on, v, jnp.zeros_like(v))
            wsrc[LATE.index(c), 0] = w
    total = ham_sum(x, lref, rref)
    g = jnp.where(inside(dims[t, 0], dims[t, 1], (width, width)), total, 0.0)
    gref[0] = g
    num = total_of(x[0].astype(F32) * g)
    sums[...] += jnp.where(srow == 0, squares, jnp.where(srow == 1, num, 0.0))


def pack_kernel(caps, src_caps, starts, coefs, vsrc, wsrc, lref, out, acc):
    t = pl.program_id(0)
    width = vsrc.shape[2]
    kinds = lref.shape[0]
    lane = lax.broadcasted_iota(jnp.int32, (width, width), 1)
    kept = []
    for i, c in enumerate(LATE):
        state = (coefs[0] * vsrc[i, 0].astype(F32) + coefs[1] * wsrc[i, 0].astype(F32)).astype(BF16)
        kept.append(jnp.where(lane < src_caps[c, t], state, jnp.zeros_like(state)))
    own = jnp.where(lane < caps[t], kept[0].astype(F32), 0.0).T.astype(BF16)
    at = jnp.int32(0)
    for i, c in enumerate(LATE):
        left = jnp.concatenate([lref[k, c, 0] for k in range(kinds)], 0)
        inner = jnp.dot(left, kept[i], preferred_element_type=F32).astype(BF16)
        inner = jnp.concatenate([inner[width * k : width * (k + 1)] for k in range(kinds)], 1)
        update = jnp.dot(own, inner, preferred_element_type=F32)
        for k in range(kinds):
            tile = at // width
            lead = at - tile * width
            turned = pltpu.roll(update[:, width * k : width * (k + 1)], lead, 1)
            acc[tile] = jnp.where(lane >= lead, turned, acc[tile])
            acc[tile + 1] = turned
            at = at + src_caps[c, t]
    high = (caps[t] + 15) // 16 * 16

    def flush(tile, carry):
        first = pl.multiple_of(starts[t] + tile * high, 16)
        out[pl.ds(first, width), :] = acc[tile].astype(BF16)
        return carry

    lax.fori_loop(0, (at + width - 1) // width, flush, 0)


def unpack_kernel(caps, src_caps, starts, first_sec, packed, lenv, so_far, out):
    del so_far
    t, g = pl.program_id(0), pl.program_id(1)
    width = out.shape[3]
    kinds = out.shape[0]

    @pl.when(first_sec[0] == 1)
    def _():
        out[...] = lenv[...]

    @pl.when(first_sec[0] == 0)
    def _():
        lane = lax.broadcasted_iota(jnp.int32, (width, width), 1)
        caps_g = [src_caps[c, t] for c in LATE]
        mine = caps_g[-1]
        at = jnp.int32(0)
        for i in range(len(LATE) - 1):
            mine = jnp.where(g == i, caps_g[i], mine)
            at = at + jnp.where(g > i, kinds * caps_g[i], 0)
        high = (caps[t] + 15) // 16 * 16
        valid = inside(caps[t], mine, (width, width))
        for k in range(kinds):
            tile = jnp.where(mine > 0, at // width, 0)
            lead = at - at // width * width
            low = packed[pl.ds(pl.multiple_of(starts[t] + tile * high, 16), width), :]
            upper = packed[pl.ds(pl.multiple_of(starts[t] + (tile + 1) * high, 16), width), :]
            both = jnp.where(lane >= lead, low.astype(F32), upper.astype(F32))
            both = pltpu.roll(both, width - lead, 1)
            out[k, 0, 0] = jnp.where(valid, both, 0.0).astype(BF16)
            at = at + mine


def early_kernel(places, count, idx, there, first_sec, *refs):
    pieces = refs[: len(places)]
    one, two, lenv, out, held, sem = refs[len(places) :]
    t, g = pl.program_id(0), pl.program_id(1)
    width = out.shape[3]
    kinds = out.shape[0]

    @pl.when((t == 0) & (g == 0))
    def _():
        for copy in load_pieces(places, pieces, held, sem):
            copy.wait()

    @pl.when(first_sec[0] == 1)
    def _():
        out[...] = lenv[...]

    for i, c in enumerate(EARLY):
        here = there[c, t] > 0

        @pl.when((first_sec[0] == 0) & (g == i) & jnp.logical_not(here))
        def _():
            out[...] = jnp.zeros_like(out)

        @pl.when((first_sec[0] == 0) & (g == i) & here)
        def _():
            sent = (one, two)[i]
            own = block_of(held, idx[0, t], count, width).astype(F32).T.astype(BF16)
            kept = block_of(held, idx[c, t], count, width)
            left = jnp.concatenate([sent[k, 0] for k in range(kinds)], 0)
            inner = jnp.dot(left, kept, preferred_element_type=F32).astype(BF16)
            inner = jnp.concatenate([inner[width * k : width * (k + 1)] for k in range(kinds)], 1)
            update = jnp.dot(own, inner, preferred_element_type=F32).astype(BF16)
            for k in range(kinds):
                out[k, 0, 0] = update[:, width * k : width * (k + 1)]


def whole(shape):
    return pl.BlockSpec(shape, lambda *a: (0,) * len(shape))


def shards(wavefunction, left_env, right_env, row_offset, sector_dims, trunc_ranks):
    start, lenv, renv = wavefunction[0], left_env[0], right_env[0]
    offsets, dims, ranks = row_offset[0], sector_dims[0], trunc_ranks[0]
    count, width = start.shape[0], start.shape[1]
    channels = lenv.shape[0]
    kinds = channels // GROUPS
    nblk, device = lax.axis_size("blk"), lax.axis_index("blk")
    body = count * width
    cells = float(count * nblk * width * width)
    lines = jnp.arange(width, dtype=jnp.int32)
    first_sec = jnp.reshape((lax.axis_index("sec") == 0).astype(jnp.int32), (1,))
    by_group = lenv.reshape((kinds, GROUPS, count, width, width))

    up_val = jnp.arange(count, dtype=jnp.int32)
    down_val = (device - offsets) % nblk
    holders = jnp.stack(
        [
            jnp.broadcast_to(device, (count,)),
            (down_val + jnp.roll(offsets, 1)) % nblk,
            (down_val + jnp.roll(offsets, -1)) % nblk,
            jnp.broadcast_to((device - 1) % nblk, (count,)),
            jnp.broadcast_to((device + 1) % nblk, (count,)),
        ]
    )
    slots = jnp.stack(
        [up_val, jnp.maximum(up_val - 1, 0), jnp.minimum(up_val + 1, count - 1), up_val, up_val]
    )
    there = jnp.stack(
        [up_val >= 0, up_val >= 1, up_val <= count - 2, down_val >= 1, down_val <= nblk - 2]
    ).astype(jnp.int32)
    idx = ((holders ^ device) * count + slots).astype(jnp.int32)

    mask_on = (lines[None, :, None] < dims[:, 0][:, None, None]) & (
        lines[None, None, :] < dims[:, 1][:, None, None]
    )
    vzero = jnp.where(mask_on, start, jnp.zeros_like(start))
    caps = jnp.minimum(dims[:, 1], ranks)
    meta = jnp.zeros((EXTRA, width), BF16).at[0, :count].set(caps.astype(BF16))
    vpieces = gathered(jnp.concatenate([vzero.reshape((body, width)), meta]))
    sent_one = onward(by_group[:, 1, 1:])
    sent_two = onward(by_group[:, 2, : count - 1])
    places = tuple((place, first) for _, place, first in vpieces)
    n = len(places)
    anywhere = pl.BlockSpec(memory_space=pl.ANY)
    env = pl.BlockSpec((channels, 1, width, width), lambda t, *s: (0, t, 0, 0))
    slot_block = pl.BlockSpec((1, width, width), lambda t, *s: (t, 0, 0))
    held = pltpu.VMEM((nblk, body + EXTRA, width), BF16)
    ham_cost = pl.CostEstimate(
        flops=4 * channels * count * width**3,
        bytes_accessed=4 * channels * count * width**2 + 8 * body * width,
        transcendentals=0,
    )

    hzero, rpay = pl.pallas_call(
        functools.partial(first_kernel, places, count),
        grid_spec=pltpu.PrefetchScalarGridSpec(
            num_scalar_prefetch=3,
            grid=(count,),
            in_specs=[anywhere] * n + [env, env],
            out_specs=[slot_block, whole((body + EXTRA, width))],
            scratch_shapes=[held, pltpu.VMEM((EXTRA, 128), F32), pltpu.SemaphoreType.DMA((n,))],
        ),
        out_shape=[
            jax.ShapeDtypeStruct((count, width, width), F32),
            jax.ShapeDtypeStruct((body + EXTRA, width), BF16),
        ],
        compiler_params=params(),
        cost_estimate=ham_cost,
        name="ham_first",
    )(idx, there, dims, *[rows for rows, _, _ in vpieces], lenv, renv)

    rpieces = gathered(rpay)
    late_block = pl.BlockSpec((len(LATE), 1, width, width), lambda t, *s: (0, t, 0, 0))
    late_shape = jax.ShapeDtypeStruct((len(LATE), count, width, width), BF16)
    gone, sums, vsrc, wsrc = pl.pallas_call(
        functools.partial(second_kernel, places, count, cells),
        grid_spec=pltpu.PrefetchScalarGridSpec(
            num_scalar_prefetch=3,
            grid=(count,),
            in_specs=[anywhere] * (2 * n) + [env, env],
            out_specs=[slot_block, whole((8, 128)), late_block, late_block],
            scratch_shapes=[
                held,
                held,
                pltpu.VMEM((nblk * EXTRA, 128), F32),
                pltpu.SemaphoreType.DMA((n,)),
                pltpu.SemaphoreType.DMA((n,)),
            ],
        ),
        out_shape=[
            jax.ShapeDtypeStruct((count, width, width), F32),
            jax.ShapeDtypeStruct((8, 128), F32),
            late_shape,
            late_shape,
        ],
        compiler_params=params(),
        cost_estimate=ham_cost,
        name="ham_second",
    )(idx, there, dims, *[rows for rows, _, _ in vpieces], *[rows for rows, _, _ in rpieces], lenv, renv)

    all_caps = extras_of(vpieces, nblk, body)[:, 0, :count].astype(jnp.int32).reshape((-1,))
    src_caps = jnp.where(there > 0, jnp.take(all_caps, idx), 0).astype(jnp.int32)

    def layout(caps, src_caps):
        high = (caps + 15) // 16 * 16
        wide = (kinds * sum(src_caps[c] for c in LATE) + width - 1) // width
        ends = jnp.cumsum(high * wide)
        return ends - high * wide, ends[-1]

    starts, rows_used = layout(caps, src_caps)

    parts = lax.all_gather(
        jnp.where(jnp.arange(8)[:, None] == 4, rows_used.astype(F32), sums), "blk", axis=0
    )
    squares, num = jnp.sum(parts[:, 0, 0]) / cells, jnp.sum(parts[:, 1, 0]) / cells
    a_zero, scale = sums[2, 0], sums[3, 0]
    beta = jnp.sqrt(squares + 1e-06)
    a_one = num / (beta * beta)
    half_gap = (a_zero - a_one) / 2.0
    ritz = (a_zero + a_one) / 2.0 - jnp.sqrt(half_gap * half_gap + beta * beta)
    gap_val = ritz - a_zero
    length = jnp.sqrt(beta * beta + gap_val * gap_val)
    from_v, from_w = beta / length * scale, gap_val / length / beta
    state_new = (from_v * vzero.astype(F32) + from_w * wsrc[0].astype(F32)).astype(BF16)
    hstate_new = (from_v * hzero + from_w * gone).astype(BF16)
    kept = jnp.where(lines[None, None, :] < ranks[:, None, None], state_new, jnp.zeros_like(state_new))

    facts = jnp.concatenate([caps[None], src_caps, idx], axis=0).astype(BF16)
    facts = jnp.zeros((EXTRA, width), BF16).at[: facts.shape[0], :count].set(facts)
    passed = onward(jnp.concatenate([kept.reshape((body, width)), facts]))
    facts = passed[body:, :count].astype(jnp.int32)
    prev_caps, prev_src, prev_idx = facts[0], facts[1 : 1 + GROUPS], facts[1 + GROUPS : 1 + 2 * GROUPS]
    prev_starts, _ = layout(prev_caps, prev_src)

    tiles = kinds * len(LATE)
    most = count * tiles * width + SLACK
    coefs = jnp.stack([from_v, from_w])
    by_slot = pl.BlockSpec((kinds, GROUPS, 1, width, width), lambda t, *s: (0, 0, t, 0, 0))
    packed = pl.pallas_call(
        pack_kernel,
        grid_spec=pltpu.PrefetchScalarGridSpec(
            num_scalar_prefetch=3,
            grid=(count,),
            in_specs=[pl.BlockSpec(memory_space=pltpu.SMEM), late_block, late_block, by_slot],
            out_specs=whole((most, width)),
            scratch_shapes=[pltpu.VMEM((tiles + 2, width, width), F32)],
        ),
        out_shape=jax.ShapeDtypeStruct((most, width), BF16),
        compiler_params=params(),
        cost_estimate=pl.CostEstimate(
            flops=4 * tiles * count * width**3, bytes_accessed=4 * channels * count * width**2, transcendentals=0
        ),
        name="pack_update",
    )(caps, src_caps, starts, coefs, vsrc, wsrc, by_group)

    length = lax.axis_size("sec")
    needed = jnp.where(lax.axis_index("sec") == length - 1, 0.0, jnp.max(parts[:, 4, 0]))
    shift = 1
    while shift < length:
        turn = [(i, (i + shift) % length) for i in range(length)]
        needed = jnp.maximum(needed, lax.ppermute(jnp.full((8, 128), needed), "sec", turn)[0, 0])
        shift *= 2

    def env_block(pick):
        return pl.BlockSpec(
            (kinds, 1, 1, width, width), lambda t, g, *s: (0, pick(g), t, 0, 0)
        )

    def env_if_first(pick):
        return pl.BlockSpec(
            (kinds, 1, 1, width, width),
            lambda t, g, *s: (0, pick(g) * s[-1][0], t * s[-1][0], 0, 0),
        )

    def early_at(g):
        return g + EARLY[0]

    def late_at(g):
        return jnp.where(g == 0, LATE[0], g + LATE[1] - 1)

    out_shape = jax.ShapeDtypeStruct(by_group.shape, BF16)

    def finish(rows):
        def branch(packed, passed, sent_one, sent_two, prev_caps, prev_src, prev_idx, prev_starts, by_group):
            arrived = onward(packed[:rows])
            kpieces = gathered(passed)
            so_far = pl.pallas_call(
                functools.partial(early_kernel, places, count),
                grid_spec=pltpu.PrefetchScalarGridSpec(
                    num_scalar_prefetch=3,
                    grid=(count, len(EARLY)),
                    in_specs=[anywhere] * n
                    + [
                        pl.BlockSpec((kinds, 1, width, width), lambda t, g, *s: (0, jnp.maximum(t - 1, 0), 0, 0)),
                        pl.BlockSpec((kinds, 1, width, width), lambda t, g, *s: (0, jnp.minimum(t, count - 2), 0, 0)),
                        env_if_first(early_at),
                    ],
                    out_specs=env_block(early_at),
                    scratch_shapes=[held, pltpu.SemaphoreType.DMA((n,))],
                ),
                out_shape=out_shape,
                compiler_params=params(),
                cost_estimate=pl.CostEstimate(
                    flops=4 * kinds * len(EARLY) * count * width**3,
                    bytes_accessed=4 * kinds * len(EARLY) * count * width**2,
                    transcendentals=0,
                ),
                name="early_update",
            )(prev_idx, prev_src, first_sec, *[r for r, _, _ in kpieces], sent_one, sent_two, by_group)
            return pl.pallas_call(
                unpack_kernel,
                grid_spec=pltpu.PrefetchScalarGridSpec(
                    num_scalar_prefetch=4,
                    grid=(count, len(LATE)),
                    in_specs=[whole((rows, width)), env_if_first(late_at), anywhere],
                    out_specs=env_block(late_at),
                ),
                out_shape=out_shape,
                input_output_aliases={6: 0},
                compiler_params=params(),
                name="unpack_update",
            )(prev_caps, prev_src, prev_starts, first_sec, arrived, by_group, so_far)

        return branch

    sizes = [most * part // 16 // 16 * 16 for part in (5, 6, 7, 8, 10, 13)] + [most]
    tier = sum((needed + SLACK > size).astype(jnp.int32) for size in sizes[:-1])
    next_left = lax.switch(
        tier,
        [finish(size) for size in sizes],
        packed, passed, sent_one, sent_two, prev_caps, prev_src, prev_idx, prev_starts, by_group,
    )
    next_left = next_left.reshape((channels, count, width, width))
    return (state_new[None], hstate_new[None], jnp.reshape(ritz, (1,)), next_left[None])


def solution(mesh):
    placed = (
        P("sec", "blk", None, None),
        P("sec", None, "blk", None, None),
        P("sec", None, "blk", None, None),
        P("sec", None),
        P("sec", "blk", None),
        P("sec", "blk"),
    )
    return jax.shard_map(
        shards,
        mesh=mesh,
        in_specs=placed,
        out_specs=(
            P("sec", "blk", None, None),
            P("sec", "blk", None, None),
            P("sec"),
            P("sec", None, "blk", None, None),
        ),
        check_vma=False,
    )
```

time: 455 us -> 226 us (0.50)
  waiting for transfers between devices: 241 us -> 56.9 us
  Pallas kernels: 0 us -> 88.2 us
  local copies, waits for them, and re-layouts: 75.1 us -> 18.8 us
  matrix products: 55.8 us -> 0 us
  blocking collectives: 40.1 us -> 8.33 us
  starting transfers between devices: 3.69 us -> 32 us
  between operations: 18.8 us -> 9.1 us
  other arithmetic: 18.8 us -> 13.6 us
    ppermute x1 -> x33, waiting for transfers between devices: 168 us -> 56.9 us  [the longest x27 25.2 us: exchange(): return lax.ppermute(value, 'blk', [(i, i ^ bit) for i in range(length)])]
    pallas_call x0 -> x5, Pallas kernels: none -> 88.2 us  [the longest x1 20.8 us: branch(): pl.pallas_call(functools.partial(early_kernel, places, count), grid_spec=...]
    all_gather x3 -> x0, waiting for transfers between devices: 72.7 us -> none  [route_blocks(): whole = lax.all_gather(state, 'blk', axis=0, tiled=True)]
    dot_general x15 -> x0, matrix products: 55.8 us -> none  [the longest x10 36.4 us: apply_ham(): jnp.einsum('wtac,wtdc->tad', inner, renv[ctype::5], preferred_element_typ...]
    psum x3 -> x0, blocking collectives: 40.1 us -> none  [the longest x1 13.9 us: shards(): a_one = lax.psum(jnp.sum(vone.astype(jnp.float32) * hone), 'blk') / cells]
    gather x12 -> x2, local copies, waits for them, and re-layouts: 30.1 us -> 0.86 us  [shards(): jnp.take(all_caps, idx)]
    ppermute x1 -> x33, starting transfers between devices: 3.38 us -> 32 us  [the longest x27 18.3 us: exchange(): return lax.ppermute(value, 'blk', [(i, i ^ bit) for i in range(length)])]
    another operation x1 -> x10, local copies, waits for them, and re-layouts: 10.7 us -> 0.12 us  [the longest x2 0.04 us: shards(): jnp.stack([up_val >= 0, up_val >= 1, up_val <= count - 2, down_val >= 1,...]
  transfers between devices with their start and end apart: 4 -> 33, of which waited for: 4 -> 10; matrix products, arithmetic and copies ran while one was open for 6% -> 11% of each run, Pallas kernels for 0% -> 24%
where the time goes in v1:
time: 226 us; the launch traced here: 227 us
  Pallas kernels  88.2 us (39%)
  waiting for transfers between devices  56.9 us (25%)
  starting transfers between devices  32 us (14%)
  local copies, waits for them, and re-layouts  18.8 us (8%)
  other arithmetic  13.6 us (6%)
  between operations  9.1 us (4%)
  blocking collectives  8.33 us (4%)
    ppermute x27, waiting for transfers between devices, exchange(): return lax.ppermute(value, 'blk', [(i, i ^ bit) for i in range(length)])  25.2 us
    pallas_call x1, Pallas kernels, branch(): pl.pallas_call(functools.partial(early_kernel, places, count), grid_spec=...  20.8 us
    ppermute x2, waiting for transfers between devices, shards(): lax.ppermute(jnp.full((8, 128), needed), 'sec', turn)[0, 0]  19.4 us
    pallas_call x1, Pallas kernels, shards(): pl.pallas_call(functools.partial(second_kernel, places, count, cells), gr...  18.6 us
    ppermute x27, starting transfers between devices, exchange(): return lax.ppermute(value, 'blk', [(i, i ^ bit) for i in range(length)])  18.3 us
    pallas_call x1, Pallas kernels, shards(): pl.pallas_call(functools.partial(first_kernel, places, count), grid_spec=...  17.4 us
    pallas_call x1, Pallas kernels, branch(): pl.pallas_call(unpack_kernel, grid_spec=pltpu.PrefetchScalarGridSpec(num_...  16.6 us
    pallas_call x1, Pallas kernels, shards(): pl.pallas_call(pack_kernel, grid_spec=pltpu.PrefetchScalarGridSpec(num_sc...  14.8 us
  transfers between devices with their start and end apart: 33, of which 10 were waited for; matrix products, arithmetic and copies ran while one was open for 11% of the time, Pallas kernels for 24%

profile of v1, /device:TPU:8, one launch (start us, length us, event | category | flops | bytes accessed | tf_op | source)
XLA Modules:
  0.0 227.1 jit_solution(5371895010038709691)
XLA Ops:
  0.6 0.8 slice_bitcast_fusion.11
  2.2 1.3 fusion.1
  3.5 1.6 collective-permute-start.73
  5.1 1.5 collective-permute-start.71
  6.6 1.3 fusion.35
  7.9 0.8 fusion.34
  8.7 1.4 copy.20.dims
  10.1 1.4 constant_dynamic-update-slice_fusion.11
  11.5 0.7 constant_dynamic-update-slice_fusion.10
  13.1 0.7 iota_compare_fusion.2
  14.5 1.6 collective-permute-start.75
  16.1 1.6 collective-permute-start.77
  18.2 3.6 %collective-permute-done.77.refs_6_ = bf16[768,128]{1,0:T(8,128)(2,1)S(1)} collective-permute-done((bf16[768,128]{1,0:T(8,128)(2,1)S(1)}, bf16[768,128]{1,0:T(8,128)(2,1)S(1)}, u32[]{:S(2)}, u32[]{:S(2)}) %collective-permute-start.77) | collective-permute-done | bytes 196640 | tf_op jit(solution)/shard_map/ppermute | solution.py:26
  22.4 1.1 collective-permute-done.76.refs_9_
  23.7 0.8 gather_fusion
  25.2 17.4 %ham_first.1 = (f32[12,128,128]{2,1,0:T(8,128)}, bf16[1552,128]{1,0:T(8,128)(2,1)}) custom-call(s32[5,12]{1,0:T(8,128)} %get-tuple-element.716.idx, s32[5,12]{1,0:T(8,128)} %convert_element_type.68.there, s32[12,2]{1,0:T(8,128)} %copy.20.dims, bf16[1552,128]{1,0:T(8,128)(2,1)} %copy-done.1, bf16[1552,128]{1,0:T(8,128)(2,1)} %copy-done.4, ...), custom_call_target="tpu_custom_call" | custom-call | flops 2013265920 | bytes 17301504 | tf_op jit(solution)/shard_map/ham_first/pallas_call | solution.py:362
  42.7 1.6 collective-permute-start.82
  44.8 3.2 %slice_bitcast_fusion = (bf16[4,11,128,128]{3,2,1,0:T(8,128)(2,1)}, bf16[4,11,128,128]{3,2,1,0:T(8,128)(2,1)S(1)}) fusion(bf16[4,5,12,128,128]{4,3,2,1,0:T(8,128)(2,1)} %bitcast.185), kind=kLoop, calls=%fused_computation.36 | loop fusion | bytes 5767168 | tf_op jit(solution)/shard_map/squeeze | solution.py:349
  48.0 6.3 %collective-permute-done.82.refs_14_ = bf16[1552,128]{1,0:T(8,128)(2,1)S(1)} collective-permute-done((bf16[1552,128]{1,0:T(8,128)(2,1)}, bf16[1552,128]{1,0:T(8,128)(2,1)S(1)}, u32[]{:S(2)}, u32[]{:S(2)}) %collective-permute-start.82) | collective-permute-done | bytes 397344 | tf_op jit(solution)/shard_map/ppermute | solution.py:26
  54.3 0.7 slice.328
  55.0 1.3 collective-permute-start.85
  57.0 0.8 collective-permute-start.84
  59.8 3.5 %collective-permute-done.84.refs_16_ = bf16[768,128]{1,0:T(8,128)(2,1)} collective-permute-done((bf16[768,128]{1,0:T(8,128)(2,1)}, bf16[768,128]{1,0:T(8,128)(2,1)}, u32[]{:S(2)}, u32[]{:S(2)}) %collective-permute-start.84) | collective-permute-done | bytes 196640 | tf_op jit(solution)/shard_map/ppermute | solution.py:26
  64.3 3.5 %collective-permute-start.92 = (bf16[4,11,128,128]{3,2,1,0:T(8,128)(2,1)}, bf16[4,11,128,128]{3,2,1,0:T(8,128)(2,1)}, u32[]{:S(2)}, u32[]{:S(2)}) collective-permute-start(bf16[4,11,128,128]{3,2,1,0:T(8,128)(2,1)} %get-tuple-element.738), channel_id=1, source_target_pairs={{0,8},{8,16},{16,24},{1,9},{9,17},{17,25},{2,10},{10,18},{18,26},{... | collective-permute-start | bytes 4325384 | tf_op jit(solution)/shard_map/ppermute | solution.py:31
  67.9 3.6 %collective-permute-start.91 = (bf16[4,11,128,128]{3,2,1,0:T(8,128)(2,1)S(1)}, bf16[4,11,128,128]{3,2,1,0:T(8,128)(2,1)}, u32[]{:S(2)}, u32[]{:S(2)}) collective-permute-start(bf16[4,11,128,128]{3,2,1,0:T(8,128)(2,1)S(1)} %get-tuple-element.739), channel_id=1, source_target_pairs={{0,8},{8,16},{16,24},{1,9},{9,17},{17,25},{2,10},{10,18},{18,26},{... | collective-permute-start | bytes 4325384 | tf_op jit(solution)/shard_map/ppermute | solution.py:31
  72.2 18.6 %ham_second.1 = (f32[12,128,128]{2,1,0:T(8,128)}, f32[8,128]{1,0:T(8,128)}, bf16[3,12,128,128]{3,2,1,0:T(8,128)(2,1)}, bf16[3,12,128,128]{3,2,1,0:T(8,128)(2,1)}) custom-call(s32[5,12]{1,0:T(8,128)} %get-tuple-element.716.idx, s32[5,12]{1,0:T(8,128)} %convert_element_type.68.there, s32[12,2]{1,0:T(8,128)} %copy.20.dims, bf16[1552,128]{1,0:T(8,128)(2,1)} %copy-done.1, ...), custom_call_target="tpu_custom_call" | custom-call | flops 2013265920 | bytes 17301504 | tf_op jit(solution)/shard_map/ham_second/pallas_call | solution.py:383
  90.9 1.3 fusion.33
  92.1 0.7 broadcast_select_fusion
  92.9 8.3 %all-gather = f32[64,128]{1,0:T(8,128)S(1)} all-gather(f32[8,128]{1,0:T(8,128)S(1)} %broadcast_select_fusion), channel_id=2, replica_groups=mesh['sec'=4,'blk'=8] {'blk'}, dimensions={0}, use_global_device_ids=true | all-gather | bytes 36864 | tf_op jit(solution)/shard_map/all_gather | solution.py:420
  106.8 2.1 convert_multiply_fusion
  109.1 1.9 collective-permute-start.90
  111.0 0.9 fusion.2
  112.5 19.4 %collective-permute-done.88 = f32[8,128]{1,0:T(8,128)S(1)} collective-permute-done((f32[8,128]{1,0:T(8,128)S(1)}, f32[8,128]{1,0:T(8,128)S(1)}, u32[]{:S(2)}, u32[]{:S(2)}) %collective-permute-start.88) | collective-permute-done | bytes 4128 | tf_op jit(solution)/shard_map/ppermute | solution.py:469
  133.2 2.7 %collective-permute-start.89 = (f32[8,128]{1,0:T(8,128)S(1)}, f32[8,128]{1,0:T(8,128)S(1)}, u32[]{:S(2)}, u32[]{:S(2)}) collective-permute-start(f32[8,128]{1,0:T(8,128)S(1)} %broadcast_in_dim.50), channel_id=1, source_target_pairs={{0,16},{8,24},{16,0},{24,8},{1,17},{9,25},{17,1},{25,9},{2,18},{10... | collective-permute-start | bytes 12296 | tf_op jit(solution)/shard_map/ppermute | solution.py:469
  135.9 14.8 %pack_update.1 = bf16[18560,128]{1,0:T(8,128)(2,1)} custom-call(s32[12]{0:T(128)} %get-tuple-element.711.caps, s32[5,12]{1,0:T(8,128)} %copy-done.83, s32[12]{0:T(128)} %get-tuple-element.710.starts, f32[2]{0:T(128)} %pad_maximum_fusion.2.coefs, bf16[3,12,128,128]{3,2,1,0:T(8,128)(2,1)} %get-tuple-element.706.vsrc, ...), custom_call_target="tpu_custom_call" | custom-call | flops 1207959552 | bytes 15728640 | tf_op jit(solution)/shard_map/pack_update/pallas_call | solution.py:447
  152.8 73.2 %conditional.1 = (bf16[1,20,12,128,128]{4,3,2,1,0:T(8,128)(2,1)}) conditional(s32[]{:T(128)} %clamp.3, (s32[16,12]{1,0:T(8,128)S(1)}, s32[12,1]{0,1:T(1,128)S(1)}, s32[12]{0:T(128)S(1)}, s32[12]{0:T(128)S(1)}, s32[12]{0:T(128)S(1)}, /*index=5*/pred[12]{0:T(512)(128)(4,1)S(1)}, s32[12]{0:T(128)S(1)}, s32[12]{0:T(128)S(1)}, ...), branch_computations={%region_5.6_spmd, %region_6.7_spmd, %region_7.8_spmd, %region_8.9_... | conditional | flops 805306624 | bytes 83945664 | solution.py:536
  152.8 2.8 %slice.209 = bf16[9280,128]{1,0:T(8,128)(2,1)} slice(bf16[18560,128]{1,0:T(8,128)(2,1)} %get-tuple-element.623), slice={[0:9280], [0:128]} | slice | bytes 4751360 | tf_op jit(solution)/shard_map/cond/branch_3_fun/slice | solution.py:493
  155.6 1.9 collective-permute-start.30
  157.5 0.8 collective-permute-start.34
  158.3 1.5 collective-permute-start.32
  159.8 6.8 %collective-permute-done.34.refs_4_ = bf16[1552,128]{1,0:T(8,128)(2,1)S(1)} collective-permute-done((bf16[1552,128]{1,0:T(8,128)(2,1)S(1)}, bf16[1552,128]{1,0:T(8,128)(2,1)S(1)}, u32[]{:S(2)}, u32[]{:S(2)}) %collective-permute-start.34) | collective-permute-done | bytes 397344 | tf_op jit(solution)/shard_map/cond/branch_3_fun/ppermute | solution.py:26
  166.7 0.8 collective-permute-start.37
  167.8 1.7 collective-permute-start.36
  170.6 2.9 %collective-permute-done.36.refs_6_ = bf16[768,128]{1,0:T(8,128)(2,1)S(1)} collective-permute-done((bf16[768,128]{1,0:T(8,128)(2,1)S(1)}, bf16[768,128]{1,0:T(8,128)(2,1)S(1)}, u32[]{:S(2)}, u32[]{:S(2)}) %collective-permute-start.36) | collective-permute-done | bytes 196640 | tf_op jit(solution)/shard_map/cond/branch_3_fun/ppermute | solution.py:26
  174.0 1.2 bitcast_subtract_fusion.3.starts
  176.3 20.8 %early_update.10.so_far = bf16[4,5,12,128,128]{4,3,2,1,0:T(8,128)(2,1)} custom-call(s32[5,12]{1,0:T(8,128)} %get-tuple-element.730.idx, s32[5,12]{1,0:T(8,128)} %get-tuple-element.731.there.src_caps, s32[1]{0:T(128)} %bitcast.10.first_sec, bf16[1552,128]{1,0:T(8,128)(2,1)S(1)} %get-tuple-element.625.refs_0_, bf16[1552,128]{1,0:T(8,128)(2,1)} %copy-done.34, ...), custom_call_target="tpu_custom_call" | custom-call | flops 805306368 | bytes 6291456 | tf_op jit(solution)/shard_map/cond/branch_3_fun/early_update/pallas_call | solution.py:495
  197.0 12.2 %collective-permute-done.30.packed = bf16[9280,128]{1,0:T(8,128)(2,1)} collective-permute-done((bf16[9280,128]{1,0:T(8,128)(2,1)}, bf16[9280,128]{1,0:T(8,128)(2,1)}, u32[]{:S(2)}, u32[]{:S(2)}) %collective-permute-start.30) | collective-permute-done | bytes 2375712 | tf_op jit(solution)/shard_map/cond/branch_3_fun/ppermute | solution.py:31
  209.3 16.6 %unpack_update.10 = bf16[4,5,12,128,128]{4,3,2,1,0:T(8,128)(2,1)} custom-call(s32[12]{0:T(128)S(1)} %get-tuple-element.607.caps, s32[5,12]{1,0:T(8,128)} %get-tuple-element.731.there.src_caps, s32[12]{0:T(128)} %bitcast_subtract_fusion.3.starts, s32[1]{0:T(128)} %bitcast.10.first_sec, ...), custom_call_target="tpu_custom_call", output_to_operand_aliasing={{}: (6, {})} | custom-call | tf_op jit(solution)/shard_map/cond/branch_3_fun/unpack_update/pallas_call | solution.py:518
  (180 shorter events, 15.0 us)
Async XLA Ops:
  3.5 21.7 %copy-start.1 = (bf16[1552,128]{1,0:T(8,128)(2,1)}, bf16[1552,128]{1,0:T(8,128)(2,1)S(1)}, u32[]{:S(2)}) copy-start(bf16[1552,128]{1,0:T(8,128)(2,1)S(1)} %pad_maximum_fusion.refs_0_) | copy-start | bytes 1191940
  3.5 11.0 %collective-permute-start.73 = (bf16[1552,128]{1,0:T(8,128)(2,1)S(1)}, bf16[1552,128]{1,0:T(8,128)(2,1)S(1)}, u32[]{:S(2)}, u32[]{:S(2)}) collective-permute-start(bf16[1552,128]{1,0:T(8,128)(2,1)S(1)} %pad_maximum_fusion.refs_0_), channel_id=1, source_target_pairs={{0,4},{1,5},{2,6},{3,7},{4,0},{5,1},{6,2},{7,3},{8,12},{9,13},{10,... | collective-permute-start | bytes 1191944 | tf_op jit(solution)/shard_map/ppermute | solution.py:26
  5.1 11.0 %collective-permute-start.71 = (bf16[1552,128]{1,0:T(8,128)(2,1)S(1)}, bf16[1552,128]{1,0:T(8,128)(2,1)S(1)}, u32[]{:S(2)}, u32[]{:S(2)}) collective-permute-start(bf16[1552,128]{1,0:T(8,128)(2,1)S(1)} %pad_maximum_fusion.refs_0_), channel_id=1, source_target_pairs={{0,2},{1,3},{2,0},{3,1},{4,6},{5,7},{6,4},{7,5},{8,10},{9,11},{10,... | collective-permute-start | bytes 1191944 | tf_op jit(solution)/shard_map/ppermute | solution.py:26
  6.6 11.6 %collective-permute-start.70 = (bf16[1552,128]{1,0:T(8,128)(2,1)S(1)}, bf16[1552,128]{1,0:T(8,128)(2,1)S(1)}, u32[]{:S(2)}, u32[]{:S(2)}) collective-permute-start(bf16[1552,128]{1,0:T(8,128)(2,1)S(1)} %pad_maximum_fusion.refs_0_), channel_id=1, source_target_pairs={{0,1},{1,0},{2,3},{3,2},{4,5},{5,4},{6,7},{7,6},{8,9},{9,8},{10,11... | collective-permute-start | bytes 1191944 | tf_op jit(solution)/shard_map/ppermute | solution.py:26
  14.5 10.6 %copy-start.2 = (bf16[1552,128]{1,0:T(8,128)(2,1)}, bf16[1552,128]{1,0:T(8,128)(2,1)S(1)}, u32[]{:S(2)}) copy-start(bf16[1552,128]{1,0:T(8,128)(2,1)S(1)} %collective-permute-done.73.refs_4_) | copy-start | bytes 1191940
  14.5 7.3 %collective-permute-start.75 = (bf16[784,128]{1,0:T(8,128)(2,1)S(1)}, bf16[784,128]{1,0:T(8,128)(2,1)S(1)}, u32[]{:S(2)}, u32[]{:S(2)}) collective-permute-start(bf16[784,128]{1,0:T(8,128)(2,1)S(1)} %slice.322), channel_id=1, source_target_pairs={{0,2},{1,3},{2,0},{3,1},{4,6},{5,7},{6,4},{7,5},{8,10},{9,11},{10,... | collective-permute-start | bytes 602120 | tf_op jit(solution)/shard_map/ppermute | solution.py:26
  16.1 9.1 %copy-start.3 = (bf16[1552,128]{1,0:T(8,128)(2,1)}, bf16[1552,128]{1,0:T(8,128)(2,1)S(1)}, u32[]{:S(2)}) copy-start(bf16[1552,128]{1,0:T(8,128)(2,1)S(1)} %collective-permute-done.71.refs_2_) | copy-start | bytes 1191940
  16.1 5.7 %collective-permute-start.77 = (bf16[768,128]{1,0:T(8,128)(2,1)S(1)}, bf16[768,128]{1,0:T(8,128)(2,1)S(1)}, u32[]{:S(2)}, u32[]{:S(2)}) collective-permute-start(bf16[768,128]{1,0:T(8,128)(2,1)S(1)} %slice.326), channel_id=1, source_target_pairs={{0,4},{1,5},{2,6},{3,7},{4,0},{5,1},{6,2},{7,3},{8,12},{9,13},{10,... | collective-permute-start | bytes 589832 | tf_op jit(solution)/shard_map/ppermute | solution.py:26
  17.7 4.7 %collective-permute-start.74 = (bf16[1552,128]{1,0:T(8,128)(2,1)S(1)}, bf16[1552,128]{1,0:T(8,128)(2,1)S(1)}, u32[]{:S(2)}, u32[]{:S(2)}) collective-permute-start(bf16[1552,128]{1,0:T(8,128)(2,1)S(1)} %collective-permute-done.73.refs_4_), channel_id=1, source_target_pairs={{0,1},{1,0},{2,3},{3,2},{4,5},{5,4},{6,7},{7,6},{8,9},{9,8},{10,11... | collective-permute-start | bytes 1191944 | tf_op jit(solution)/shard_map/ppermute | solution.py:26
  17.7 4.7 %collective-permute-start.72 = (bf16[1552,128]{1,0:T(8,128)(2,1)S(1)}, bf16[1552,128]{1,0:T(8,128)(2,1)S(1)}, u32[]{:S(2)}, u32[]{:S(2)}) collective-permute-start(bf16[1552,128]{1,0:T(8,128)(2,1)S(1)} %collective-permute-done.71.refs_2_), channel_id=1, source_target_pairs={{0,1},{1,0},{2,3},{3,2},{4,5},{5,4},{6,7},{7,6},{8,9},{9,8},{10,11... | collective-permute-start | bytes 1191944 | tf_op jit(solution)/shard_map/ppermute | solution.py:26
  21.8 3.3 %collective-permute-start.78 = (bf16[768,128]{1,0:T(8,128)(2,1)S(1)}, bf16[768,128]{1,0:T(8,128)(2,1)}, u32[]{:S(2)}, u32[]{:S(2)}) collective-permute-start(bf16[768,128]{1,0:T(8,128)(2,1)S(1)} %collective-permute-done.77.refs_6_), channel_id=1, source_target_pairs={{0,1},{1,0},{2,3},{3,2},{4,5},{5,4},{6,7},{7,6},{8,9},{9,8},{10,11... | collective-permute-start | bytes 589832 | tf_op jit(solution)/shard_map/ppermute | solution.py:26
  21.9 1.7 collective-permute-start.76
  25.1 33.2 %copy-start.83 = (s32[5,12]{1,0:T(8,128)}, s32[5,12]{1,0:T(8,128)S(1)}, u32[]{:S(2)}) copy-start(s32[5,12]{1,0:T(8,128)S(1)} %get-tuple-element.715.src_caps) | copy-start | bytes 724
  42.6 15.7 %copy-start.84 = (s32[1,12,2]{1,2,0:T(2,128)S(1)}, s32[1,12,2]{1,2,0:T(2,128)}, u32[]{:S(2)}) copy-start(s32[1,12,2]{1,2,0:T(2,128)} %param.21) | copy-start | bytes 292
  42.7 15.7 %copy-start.85 = (s32[1,12]{1,0:T(1,128)S(1)}, s32[1,12]{1,0:T(1,128)}, u32[]{:S(2)}) copy-start(s32[1,12]{1,0:T(1,128)} %param.22) | copy-start | bytes 148
  42.7 15.7 %copy-start.82 = (s32[5,12]{1,0:T(8,128)S(1)}, s32[5,12]{1,0:T(8,128)}, u32[]{:S(2)}) copy-start(s32[5,12]{1,0:T(8,128)} %get-tuple-element.716.idx) | copy-start | bytes 724
  42.7 11.6 %collective-permute-start.82 = (bf16[1552,128]{1,0:T(8,128)(2,1)}, bf16[1552,128]{1,0:T(8,128)(2,1)S(1)}, u32[]{:S(2)}, u32[]{:S(2)}) collective-permute-start(bf16[1552,128]{1,0:T(8,128)(2,1)} %get-tuple-element.701.refs_10_), channel_id=1, source_target_pairs={{0,4},{1,5},{2,6},{3,7},{4,0},{5,1},{6,2},{7,3},{8,12},{9,13},{10,... | collective-permute-start | bytes 1191944 | tf_op jit(solution)/shard_map/ppermute | solution.py:26
  44.3 12.0 %collective-permute-start.80 = (bf16[1552,128]{1,0:T(8,128)(2,1)}, bf16[1552,128]{1,0:T(8,128)(2,1)S(1)}, u32[]{:S(2)}, u32[]{:S(2)}) collective-permute-start(bf16[1552,128]{1,0:T(8,128)(2,1)} %get-tuple-element.701.refs_10_), channel_id=1, source_target_pairs={{0,2},{1,3},{2,0},{3,1},{4,6},{5,7},{6,4},{7,5},{8,10},{9,11},{10,... | collective-permute-start | bytes 1191944 | tf_op jit(solution)/shard_map/ppermute | solution.py:26
  48.0 16.4 %collective-permute-start.79 = (bf16[1552,128]{1,0:T(8,128)(2,1)S(1)}, bf16[1552,128]{1,0:T(8,128)(2,1)S(1)}, u32[]{:S(2)}, u32[]{:S(2)}) collective-permute-start(bf16[1552,128]{1,0:T(8,128)(2,1)S(1)} %copy-done.29), channel_id=1, source_target_pairs={{0,1},{1,0},{2,3},{3,2},{4,5},{5,4},{6,7},{7,6},{8,9},{9,8},{10,11... | collective-permute-start | bytes 1191944 | tf_op jit(solution)/shard_map/ppermute | solution.py:26
  54.3 17.2 %copy-start.8 = (bf16[1552,128]{1,0:T(8,128)(2,1)}, bf16[1552,128]{1,0:T(8,128)(2,1)S(1)}, u32[]{:S(2)}) copy-start(bf16[1552,128]{1,0:T(8,128)(2,1)S(1)} %collective-permute-done.82.refs_14_) | copy-start | bytes 1191940
  55.0 8.3 %collective-permute-start.85 = (bf16[784,128]{1,0:T(8,128)(2,1)}, bf16[784,128]{1,0:T(8,128)(2,1)}, u32[]{:S(2)}, u32[]{:S(2)}) collective-permute-start(bf16[784,128]{1,0:T(8,128)(2,1)} %slice.328), channel_id=1, source_target_pairs={{0,2},{1,3},{2,0},{3,1},{4,6},{5,7},{6,4},{7,5},{8,10},{9,11},{10,... | collective-permute-start | bytes 602120 | tf_op jit(solution)/shard_map/ppermute | solution.py:26
  56.3 15.2 %copy-start.16 = (bf16[1552,128]{1,0:T(8,128)(2,1)}, bf16[1552,128]{1,0:T(8,128)(2,1)S(1)}, u32[]{:S(2)}) copy-start(bf16[1552,128]{1,0:T(8,128)(2,1)S(1)} %collective-permute-done.80.refs_12_) | copy-start | bytes 1191940
  57.0 6.3 %collective-permute-start.84 = (bf16[768,128]{1,0:T(8,128)(2,1)}, bf16[768,128]{1,0:T(8,128)(2,1)}, u32[]{:S(2)}, u32[]{:S(2)}) collective-permute-start(bf16[768,128]{1,0:T(8,128)(2,1)} %slice.327), channel_id=1, source_target_pairs={{0,4},{1,5},{2,6},{3,7},{4,0},{5,1},{6,2},{7,3},{8,12},{9,13},{10,... | collective-permute-start | bytes 589832 | tf_op jit(solution)/shard_map/ppermute | solution.py:26
  57.8 13.7 %collective-permute-start.83 = (bf16[1552,128]{1,0:T(8,128)(2,1)S(1)}, bf16[1552,128]{1,0:T(8,128)(2,1)}, u32[]{:S(2)}, u32[]{:S(2)}) collective-permute-start(bf16[1552,128]{1,0:T(8,128)(2,1)S(1)} %collective-permute-done.82.refs_14_), channel_id=1, source_target_pairs={{0,1},{1,0},{2,3},{3,2},{4,5},{5,4},{6,7},{7,6},{8,9},{9,8},{10,11... | collective-permute-start | bytes 1191944 | tf_op jit(solution)/shard_map/ppermute | solution.py:26
  57.8 13.7 %collective-permute-start.81 = (bf16[1552,128]{1,0:T(8,128)(2,1)S(1)}, bf16[1552,128]{1,0:T(8,128)(2,1)}, u32[]{:S(2)}, u32[]{:S(2)}) collective-permute-start(bf16[1552,128]{1,0:T(8,128)(2,1)S(1)} %collective-permute-done.80.refs_12_), channel_id=1, source_target_pairs={{0,1},{1,0},{2,3},{3,2},{4,5},{5,4},{6,7},{7,6},{8,9},{9,8},{10,11... | collective-permute-start | bytes 1191944 | tf_op jit(solution)/shard_map/ppermute | solution.py:26
  63.3 4.5 %collective-permute-start.86 = (bf16[768,128]{1,0:T(8,128)(2,1)}, bf16[768,128]{1,0:T(8,128)(2,1)S(1)}, u32[]{:S(2)}, u32[]{:S(2)}) collective-permute-start(bf16[768,128]{1,0:T(8,128)(2,1)} %collective-permute-done.84.refs_16_), channel_id=1, source_target_pairs={{0,1},{1,0},{2,3},{3,2},{4,5},{5,4},{6,7},{7,6},{8,9},{9,8},{10,11... | collective-permute-start | bytes 589832 | tf_op jit(solution)/shard_map/ppermute | solution.py:26
  63.3 8.2 %collective-permute-start.87 = (bf16[784,128]{1,0:T(8,128)(2,1)}, bf16[784,128]{1,0:T(8,128)(2,1)S(1)}, u32[]{:S(2)}, u32[]{:S(2)}) collective-permute-start(bf16[784,128]{1,0:T(8,128)(2,1)} %collective-permute-done.85.refs_17_), channel_id=1, source_target_pairs={{0,1},{1,0},{2,3},{3,2},{4,5},{5,4},{6,7},{7,6},{8,9},{9,8},{10,11... | collective-permute-start | bytes 602120 | tf_op jit(solution)/shard_map/ppermute | solution.py:26
  64.3 87.8 %collective-permute-start.92 = (bf16[4,11,128,128]{3,2,1,0:T(8,128)(2,1)}, bf16[4,11,128,128]{3,2,1,0:T(8,128)(2,1)}, u32[]{:S(2)}, u32[]{:S(2)}) collective-permute-start(bf16[4,11,128,128]{3,2,1,0:T(8,128)(2,1)} %get-tuple-element.738), channel_id=1, source_target_pairs={{0,8},{8,16},{16,24},{1,9},{9,17},{17,25},{2,10},{10,18},{18,26},{... | collective-permute-start | bytes 4325384 | tf_op jit(solution)/shard_map/ppermute | solution.py:31
  67.9 38.9 %copy-start.7 = (bf16[1,12,128,128]{3,2,1,0:T(8,128)(2,1)S(1)}, bf16[1,12,128,128]{3,2,1,0:T(8,128)(2,1)}, u32[]{:S(2)}) copy-start(bf16[1,12,128,128]{3,2,1,0:T(8,128)(2,1)} %param.17) | copy-start | bytes 1179652
  67.9 84.3 %collective-permute-start.91 = (bf16[4,11,128,128]{3,2,1,0:T(8,128)(2,1)S(1)}, bf16[4,11,128,128]{3,2,1,0:T(8,128)(2,1)}, u32[]{:S(2)}, u32[]{:S(2)}) collective-permute-start(bf16[4,11,128,128]{3,2,1,0:T(8,128)(2,1)S(1)} %get-tuple-element.739), channel_id=1, source_target_pairs={{0,8},{8,16},{16,24},{1,9},{9,17},{17,25},{2,10},{10,18},{18,26},{... | collective-permute-start | bytes 4325384 | tf_op jit(solution)/shard_map/ppermute | solution.py:31
  90.9 20.2 %copy-start.27 = (f32[12,128,128]{2,1,0:T(8,128)S(1)}, f32[12,128,128]{2,1,0:T(8,128)}, u32[]{:S(2)}) copy-start(f32[12,128,128]{2,1,0:T(8,128)} %get-tuple-element.704) | copy-start | bytes 2359300
  106.0 25.9 %collective-permute-start.88 = (f32[8,128]{1,0:T(8,128)S(1)}, f32[8,128]{1,0:T(8,128)S(1)}, u32[]{:S(2)}, u32[]{:S(2)}) collective-permute-start(f32[8,128]{1,0:T(8,128)S(1)} %broadcast_in_dim.49), channel_id=1, source_target_pairs={{0,8},{8,16},{16,24},{24,0},{1,9},{9,17},{17,25},{25,1},{2,10},{10... | collective-permute-start | bytes 12296 | tf_op jit(solution)/shard_map/ppermute | solution.py:469
  109.1 42.8 %collective-permute-start.90 = (bf16[1552,128]{1,0:T(8,128)(2,1)S(1)}, bf16[1552,128]{1,0:T(8,128)(2,1)S(1)}, u32[]{:S(2)}, u32[]{:S(2)}) collective-permute-start(bf16[1552,128]{1,0:T(8,128)(2,1)S(1)} %pad_maximum_fusion.1), channel_id=1, source_target_pairs={{0,8},{8,16},{16,24},{1,9},{9,17},{17,25},{2,10},{10,18},{18,26},{... | collective-permute-start | bytes 1191944 | tf_op jit(solution)/shard_map/ppermute | solution.py:31
  133.2 17.5 %collective-permute-start.89 = (f32[8,128]{1,0:T(8,128)S(1)}, f32[8,128]{1,0:T(8,128)S(1)}, u32[]{:S(2)}, u32[]{:S(2)}) collective-permute-start(f32[8,128]{1,0:T(8,128)S(1)} %broadcast_in_dim.50), channel_id=1, source_target_pairs={{0,16},{8,24},{16,0},{24,8},{1,17},{9,25},{17,1},{25,9},{2,18},{10... | collective-permute-start | bytes 12296 | tf_op jit(solution)/shard_map/ppermute | solution.py:469
  155.6 53.7 %collective-permute-start.30 = (bf16[9280,128]{1,0:T(8,128)(2,1)}, bf16[9280,128]{1,0:T(8,128)(2,1)}, u32[]{:S(2)}, u32[]{:S(2)}) collective-permute-start(bf16[9280,128]{1,0:T(8,128)(2,1)} %slice.209), channel_id=1, source_target_pairs={{0,8},{8,16},{16,24},{1,9},{9,17},{17,25},{2,10},{10,18},{18,26},{... | collective-permute-start | bytes 7127048 | tf_op jit(solution)/shard_map/cond/branch_3_fun/ppermute | solution.py:31
  157.5 9.2 %collective-permute-start.34 = (bf16[1552,128]{1,0:T(8,128)(2,1)S(1)}, bf16[1552,128]{1,0:T(8,128)(2,1)S(1)}, u32[]{:S(2)}, u32[]{:S(2)}) collective-permute-start(bf16[1552,128]{1,0:T(8,128)(2,1)S(1)} %get-tuple-element.625.refs_0_), channel_id=1, source_target_pairs={{0,4},{1,5},{2,6},{3,7},{4,0},{5,1},{6,2},{7,3},{8,12},{9,13},{10,... | collective-permute-start | bytes 1191944 | tf_op jit(solution)/shard_map/cond/branch_3_fun/ppermute | solution.py:26
  158.3 9.4 %collective-permute-start.32 = (bf16[1552,128]{1,0:T(8,128)(2,1)S(1)}, bf16[1552,128]{1,0:T(8,128)(2,1)S(1)}, u32[]{:S(2)}, u32[]{:S(2)}) collective-permute-start(bf16[1552,128]{1,0:T(8,128)(2,1)S(1)} %get-tuple-element.625.refs_0_), channel_id=1, source_target_pairs={{0,2},{1,3},{2,0},{3,1},{4,6},{5,7},{6,4},{7,5},{8,10},{9,11},{10,... | collective-permute-start | bytes 1191944 | tf_op jit(solution)/shard_map/cond/branch_3_fun/ppermute | solution.py:26
  159.8 9.7 %collective-permute-start.31 = (bf16[1552,128]{1,0:T(8,128)(2,1)S(1)}, bf16[1552,128]{1,0:T(8,128)(2,1)S(1)}, u32[]{:S(2)}, u32[]{:S(2)}) collective-permute-start(bf16[1552,128]{1,0:T(8,128)(2,1)S(1)} %get-tuple-element.625.refs_0_), channel_id=1, source_target_pairs={{0,1},{1,0},{2,3},{3,2},{4,5},{5,4},{6,7},{7,6},{8,9},{9,8},{10,11... | collective-permute-start | bytes 1191944 | tf_op jit(solution)/shard_map/cond/branch_3_fun/ppermute | solution.py:26
  166.7 8.6 %copy-start.12 = (bf16[1552,128]{1,0:T(8,128)(2,1)}, bf16[1552,128]{1,0:T(8,128)(2,1)S(1)}, u32[]{:S(2)}) copy-start(bf16[1552,128]{1,0:T(8,128)(2,1)S(1)} %collective-permute-done.34.refs_4_) | copy-start | bytes 1191940 | tf_op jit(solution)/shard_map/cond
  166.7 6.8 %collective-permute-start.37 = (bf16[784,128]{1,0:T(8,128)(2,1)S(1)}, bf16[784,128]{1,0:T(8,128)(2,1)S(1)}, u32[]{:S(2)}, u32[]{:S(2)}) collective-permute-start(bf16[784,128]{1,0:T(8,128)(2,1)S(1)} %slice.310), channel_id=1, source_target_pairs={{0,2},{1,3},{2,0},{3,1},{4,6},{5,7},{6,4},{7,5},{8,10},{9,11},{10,... | collective-permute-start | bytes 602120 | tf_op jit(solution)/shard_map/cond/branch_3_fun/ppermute | solution.py:26
  167.8 7.5 %copy-start.20 = (bf16[1552,128]{1,0:T(8,128)(2,1)}, bf16[1552,128]{1,0:T(8,128)(2,1)S(1)}, u32[]{:S(2)}) copy-start(bf16[1552,128]{1,0:T(8,128)(2,1)S(1)} %collective-permute-done.32.refs_2_) | copy-start | bytes 1191940 | tf_op jit(solution)/shard_map/cond
  167.8 5.7 %collective-permute-start.36 = (bf16[768,128]{1,0:T(8,128)(2,1)S(1)}, bf16[768,128]{1,0:T(8,128)(2,1)S(1)}, u32[]{:S(2)}, u32[]{:S(2)}) collective-permute-start(bf16[768,128]{1,0:T(8,128)(2,1)S(1)} %slice.309), channel_id=1, source_target_pairs={{0,4},{1,5},{2,6},{3,7},{4,0},{5,1},{6,2},{7,3},{8,12},{9,13},{10,... | collective-permute-start | bytes 589832 | tf_op jit(solution)/shard_map/cond/branch_3_fun/ppermute | solution.py:26
  169.5 5.7 %collective-permute-start.35 = (bf16[1552,128]{1,0:T(8,128)(2,1)S(1)}, bf16[1552,128]{1,0:T(8,128)(2,1)S(1)}, u32[]{:S(2)}, u32[]{:S(2)}) collective-permute-start(bf16[1552,128]{1,0:T(8,128)(2,1)S(1)} %collective-permute-done.34.refs_4_), channel_id=1, source_target_pairs={{0,1},{1,0},{2,3},{3,2},{4,5},{5,4},{6,7},{7,6},{8,9},{9,8},{10,11... | collective-permute-start | bytes 1191944 | tf_op jit(solution)/shard_map/cond/branch_3_fun/ppermute | solution.py:26
  169.5 5.7 %collective-permute-start.33 = (bf16[1552,128]{1,0:T(8,128)(2,1)S(1)}, bf16[1552,128]{1,0:T(8,128)(2,1)S(1)}, u32[]{:S(2)}, u32[]{:S(2)}) collective-permute-start(bf16[1552,128]{1,0:T(8,128)(2,1)S(1)} %collective-permute-done.32.refs_2_), channel_id=1, source_target_pairs={{0,1},{1,0},{2,3},{3,2},{4,5},{5,4},{6,7},{7,6},{8,9},{9,8},{10,11... | collective-permute-start | bytes 1191944 | tf_op jit(solution)/shard_map/cond/branch_3_fun/ppermute | solution.py:26
  173.5 1.7 collective-permute-start.38
  173.5 1.7 collective-permute-start.39
  176.3 33.0 %slice-start.6 = ((s8[7864320]{0:T(1024)(128)(4,1)}), s8[4194304]{0:T(1024)(128)(4,1)S(1)}, s32[]{:S(2)}) async-start(s8[7864320]{0:T(1024)(128)(4,1)} %bitcast.201), calls=%async_computation.6 | async-start | bytes 8388608 | tf_op jit(solution)/shard_map/cond
  176.3 33.0 %slice-start.7 = ((s8[7864320]{0:T(1024)(128)(4,1)}), s8[3670016]{0:T(1024)(128)(4,1)S(1)}, s32[]{:S(2)}) async-start(s8[7864320]{0:T(1024)(128)(4,1)} %bitcast.201), calls=%async_computation.7 | async-start | bytes 7340032 | tf_op jit(solution)/shard_map/cond
  (18 other events, 51.3 us)
